TPU v7x, 256 devices: a whole 4x4x8 slice. The times are simulated.
256 devices in a mesh: pop: 32 (over y_lo, z, core), fsdp: 8 (over y_hi, x).
Axes of the slice: x: 4, y: 4 (y_hi: 2, y_lo: 2; y = y_hi * 2 + y_lo), z: 8, core: 2. Of those that a mesh axis runs over, the one named last changes fastest.
Arguments:
- tokens: bfloat16 [28672, 4096], P('pop', 'fsdp'), may hold values from -6 to 6
- up_weight: bfloat16 [4096, 14336], P('pop', 'fsdp'), may hold values from -0.09375 to 0.09375
- a_bank: bfloat16 [1024, 4096], P(None, 'pop'), may hold values from -6 to 6
- b_bank: bfloat16 [1024, 14336], P(None, 'fsdp'), may hold values from -6 to 6
- factor_index: int32 [64, 4], replicated, may hold values from 0 to 1023
- mirror: int32 [64], P('pop'), may hold values 0 or 1
- rewards: int32 [64], P('pop'), may hold values from -8 to 7
Outputs:
- hidden: bfloat16 [28672, 14336], P('pop', 'fsdp')
- update: float32 [4096, 14336], P('pop', 'fsdp')
All inputs are finite; a program needn't handle non-finite values. No bound on the sum of `mirror` on one device may be relied on, other than what follows from the above.
Results may differ from a plain program's by a relative error of at most 0.001.
Values may be sent and summed in bfloat16 or wider, within the bound.
A program may use at most 128 MiB of HBM per device.

v0:
```python
import math
import jax
import jax.numpy as jnp
from jax import lax
from jax.sharding import PartitionSpec as P

D = 4096
RANK = 4
SEQ = 448
noise_scale = 0.5


def sent_to_all(array, axis):
    copies = jnp.broadcast_to(array, (lax.axis_size(axis), *array.shape))
    return lax.all_to_all(copies, axis, split_axis=0, concat_axis=0, tiled=True)


def joined_along(parts, dim):
    parts = jnp.moveaxis(parts, 0, dim)
    dims = parts.shape
    return parts.reshape(*dims[:dim], dims[dim] * dims[dim + 1], *dims[dim + 2 :])


def gather_directly(array, axis, dim):
    parts = sent_to_all(array, axis)
    return joined_along(parts, dim)


def shaped_weights(rewards, mirror):
    members_all = rewards.shape[0]
    member_ids = jnp.arange(members_all)
    beaten = rewards[None, :] < rewards[:, None]
    level_tie = (rewards[None, :] == rewards[:, None]) & (member_ids[None, :] < member_ids[:, None])
    standing = jnp.sum((beaten | level_tie).astype(jnp.int32), axis=1)
    signed = (2 * mirror - 1).astype(jnp.float32)
    shaped = 2.0 * standing.astype(jnp.float32) / (members_all - 1) - 1.0
    return shaped * signed / math.sqrt(members_all * RANK)


def per_device(tokens, up_weight, a_bank, b_bank, factor_index, mirror, rewards):
    members_here = mirror.shape[0]
    own_width = members_here * RANK
    position = lax.axis_index("pop")
    flat_index = factor_index.reshape(-1)
    picked_a = jnp.take(a_bank, flat_index, axis=0)
    picked_b = jnp.take(b_bank, flat_index, axis=0)
    first_own = position * own_width
    gathered_a, rewards_all, mirror_all = (
        gather_directly(picked_a, "pop", 1),
        gather_directly(rewards, "pop", 0),
        gather_directly(mirror, "pop", 0),
    )
    own_a = lax.dynamic_slice_in_dim(gathered_a, first_own, own_width, 0)
    own_b = lax.dynamic_slice_in_dim(picked_b, first_own, own_width, 0).astype(jnp.float32)
    own_signs = (2 * mirror - 1).astype(jnp.float32)
    column_factor = jnp.repeat(noise_scale / math.sqrt(D * RANK) * own_signs, RANK)
    member_of_column = jnp.arange(own_width) // RANK
    row_count = tokens.shape[0]
    entire_weight = lax.all_gather(up_weight, "pop", axis=0, tiled=True)
    piece = lax.all_gather(tokens, "fsdp", axis=1, tiled=True)
    dense_sum = jnp.dot(piece, entire_weight, preferred_element_type=jnp.float32)
    low_sum = jnp.dot(piece, own_a.T, preferred_element_type=jnp.float32)
    member_of_row = jnp.arange(row_count) // SEQ
    same_member = member_of_row[:, None] == member_of_column[None, :]
    scaled = jnp.where(same_member, low_sum * column_factor[None, :], 0.0)
    perturbed = jnp.dot(scaled, own_b, precision=lax.Precision.HIGHEST)
    hidden = (dense_sum + perturbed).astype(jnp.bfloat16)
    weighting = shaped_weights(rewards_all, mirror_all)
    spread = jnp.repeat(weighting, RANK)
    update = jnp.dot(
        picked_a.astype(jnp.float32).T,
        spread[:, None] * picked_b.astype(jnp.float32),
        precision=lax.Precision.HIGHEST,
    )
    return (hidden, update)


def solution(mesh):
    in_specs = (
        P("pop", "fsdp"),
        P("pop", "fsdp"),
        P(None, "pop"),
        P(None, "fsdp"),
        P(),
        P("pop"),
        P("pop"),
    )
    out_specs = (P("pop", "fsdp"), P("pop", "fsdp"))
    return jax.shard_map(
        per_device, mesh=mesh, in_specs=in_specs, out_specs=out_specs, check_vma=False
    )
```

profile of v0, /device:TPU:1, one launch (start us, length us, event | category | flops | bytes accessed | tf_op | source)
XLA Modules:
  0.0 262.1 jit_solution(9321200983050298536)
XLA Ops:
  7.2 0.0 copy-start
  7.2 0.0 copy-start.1
  7.2 0.0 all-gather.3.cloned.1.call-start
  7.2 0.7 all-gather.3.cloned.1.call-update
  7.9 0.0 all-gather.5.cloned.1.call-start
  8.0 0.7 all-gather.5.cloned.1.call-update
  8.7 1.3 broadcast_in_dim.51
  9.9 11.1 %all-to-all-start.2 = ((s32[32,1,2]{2,1,0:T(1,128)}), s32[32,1,2]{2,1,0:T(1,128)S(1)}, u32[]{:S(2)}, u32[]{:S(2)}) async-start(s32[32,1,2]{2,1,0:T(1,128)} %broadcast_in_dim.51), calls=%async_computation.2 | async-start | bytes 32768 | tf_op jit(solution)/shard_map/all_to_all | solution.py:15
  21.1 0.8 copy.15
  21.9 0.1 reshape.94
  22.0 0.1 reshape.93
  22.1 0.0 copy-done
  22.1 0.9 gather_fusion
  23.0 5.9 %all-to-all-done.2 = s32[32,1,2]{2,1,0:T(1,128)S(1)} async-done(((s32[32,1,2]{2,1,0:T(1,128)}), s32[32,1,2]{2,1,0:T(1,128)S(1)}, u32[]{:S(2)}, u32[]{:S(2)}) %all-to-all-start.2) | async-done | bytes 288 | tf_op jit(solution)/shard_map/all_to_all | solution.py:15
  28.9 1.3 broadcast_in_dim.50
  30.1 4.3 %all-to-all-start.1 = ((s32[32,1,2]{2,1,0:T(1,128)}), s32[32,1,2]{2,1,0:T(1,128)S(1)}, u32[]{:S(2)}, u32[]{:S(2)}) async-start(s32[32,1,2]{2,1,0:T(1,128)} %broadcast_in_dim.50), calls=%async_computation.1 | async-start | bytes 32768 | tf_op jit(solution)/shard_map/all_to_all | solution.py:15
  34.4 0.1 broadcast_select_fusion.1
  34.5 0.1 copy.17
  34.6 7.6 %all-to-all-done.1 = s32[32,1,2]{2,1,0:T(1,128)S(1)} async-done(((s32[32,1,2]{2,1,0:T(1,128)}), s32[32,1,2]{2,1,0:T(1,128)S(1)}, u32[]{:S(2)}, u32[]{:S(2)}) %all-to-all-start.1) | async-done | bytes 288 | tf_op jit(solution)/shard_map/all_to_all | solution.py:15
  42.3 1.6 broadcast_in_dim.45
  43.8 4.5 %all-to-all-start = ((bf16[32,256,128]{1,2,0:T(8,128)(2,1)}), bf16[32,256,128]{1,2,0:T(8,128)(2,1)S(1)}, u32[]{:S(2)}, u32[]{:S(2)}) async-start(bf16[32,256,128]{1,2,0:T(8,128)(2,1)} %broadcast_in_dim.45), calls=%async_computation | async-start | bytes 4194304 | tf_op jit(solution)/shard_map/all_to_all | solution.py:15
  48.3 0.0 copy-done.1
  48.3 0.1 broadcast_in_dim.46
  48.4 0.1 mul.47
  48.5 5.6 %gather_fusion.1 = bf16[256,1792]{1,0:T(8,128)(2,1)} fusion(bf16[1024,1792]{1,0:T(8,128)(2,1)} %param.10, s32[1024]{0:T(1024)S(1)} %pad_clamp_fusion), kind=kCustom, calls=%fused_computation.1 | custom fusion | bytes 1836032 | tf_op jit(solution)/shard_map/jit(_take)/gather | solution.py:46
  54.1 1.3 broadcast_select_fusion
  55.4 0.1 convert_reduce_fusion.1
  55.5 0.1 convert_element_type.28
  55.6 0.5 broadcast.138
  56.1 0.7 reduce.7
  56.8 0.1 lt.62
  56.9 0.2 convert_reduce_fusion
  57.1 0.1 broadcast_in_dim.52
  57.2 0.1 mul.54
  57.3 1.9 fusion
  59.2 38.7 %all-to-all-done = bf16[32,256,128]{1,2,0:T(8,128)(2,1)S(1)} async-done(((bf16[32,256,128]{1,2,0:T(8,128)(2,1)}), bf16[32,256,128]{1,2,0:T(8,128)(2,1)S(1)}, u32[]{:S(2)}, u32[]{:S(2)}) %all-to-all-start) | async-done | bytes 2097184 | tf_op jit(solution)/shard_map/all_to_all | solution.py:15
  97.9 45.3 %all-gather.3.cloned.1.call-done = bf16[896,4096]{1,0:T(8,128)(2,1)} async-done(((bf16[896,512]{1,0:T(8,128)(2,1)}), bf16[896,4096]{1,0:T(8,128)(2,1)}) %all-gather.3.cloned.1.call-update) | async-done | bytes 7340048 | tf_op jit(solution)/shard_map/all_gather | solution.py:60
  143.3 5.6 %fusion.4 = f32[896,8]{0,1:T(8,128)S(1)} fusion(bf16[896,4096]{1,0:T(8,128)(2,1)} %all-gather.3.cloned.1.call-done, bf16[256,4096]{0,1:T(8,128)(2,1)S(1)} %bitcast.13, s32[]{:T(128)S(6)} %select_n.57, f32[8]{0:T(128)S(1)} %mul.47, s32[896]{0:T(1024)S(1)} %add_select_fusion, s32[8]{0:T(128)S(1)} %and_select_fusion), kind=kOutput, calls=%fused_computation.8 | convolution fusion | flops 58741760 | bytes 8422404 | tf_op jit(solution)/shard_map/dot_general | solution.py:62
  148.9 84.6 %all-gather.5.cloned.1.call-done = bf16[4096,1792]{1,0:T(8,128)(2,1)} async-done(((bf16[128,1792]{1,0:T(8,128)(2,1)}), bf16[4096,1792]{1,0:T(8,128)(2,1)}) %all-gather.5.cloned.1.call-update) | async-done | bytes 14680080 | tf_op jit(solution)/shard_map/all_gather | solution.py:59
  233.5 17.0 %fusion.15 = f32[896,1792]{1,0:T(8,128)S(1)} fusion(bf16[896,4096]{1,0:T(8,128)(2,1)} %all-gather.3.cloned.1.call-done, bf16[4096,1792]{1,0:T(8,128)(2,1)} %all-gather.5.cloned.1.call-done), kind=kOutput, calls=%fused_computation.38 | convolution fusion | flops 13153337344 | bytes 28442624 | tf_op jit(solution)/shard_map/dot_general | solution.py:61
  250.5 4.7 %add_convert_fusion = bf16[896,1792]{1,0:T(8,128)(2,1)} fusion(f32[896,1792]{1,0:T(8,128)S(1)} %fusion.15, f32[896,8]{0,1:T(8,128)S(1)} %fusion.4, bf16[256,1792]{1,0:T(8,128)(2,1)S(1)} %broadcast_select_fusion, s32[]{:T(128)S(6)} %select_n.57), kind=kOutput, calls=%fused_computation.2 | convolution fusion | flops 157351936 | bytes 9691140 | tf_op jit(solution)/shard_map/dot_general | solution.py:66
  (7 shorter events, 0.0 us)
Async XLA Ops:
  7.2 15.0 %copy-start = (bf16[1024,128]{1,0:T(8,128)(2,1)S(1)}, bf16[1024,128]{1,0:T(8,128)(2,1)}, u32[]{:S(2)}) copy-start(bf16[1024,128]{1,0:T(8,128)(2,1)} %param.9) | copy-start | bytes 786436
  7.2 41.1 %copy-start.1 = (s32[2]{0:T(128)S(1)}, s32[2]{0:T(128)}, u32[]{:S(2)}) copy-start(s32[2]{0:T(128)} %param.12) | copy-start | bytes 28
  7.2 136.1 %all-gather.3.cloned.1.call-start = ((), (), s32[]{:S(2)}) async-start(), calls=%async_computation.3 | async-start | bytes 8257536 | tf_op jit(solution)/shard_map/all_gather | solution.py:60
  7.9 225.6 %all-gather.5.cloned.1.call-start = ((), (), s32[]{:S(2)}) async-start(), calls=%async_computation.4 | async-start | bytes 15138816 | tf_op jit(solution)/shard_map/all_gather | solution.py:59
  9.9 18.9 %all-to-all-start.2 = ((s32[32,1,2]{2,1,0:T(1,128)}), s32[32,1,2]{2,1,0:T(1,128)S(1)}, u32[]{:S(2)}, u32[]{:S(2)}) async-start(s32[32,1,2]{2,1,0:T(1,128)} %broadcast_in_dim.51), calls=%async_computation.2 | async-start | bytes 32768 | tf_op jit(solution)/shard_map/all_to_all | solution.py:15
  30.1 12.2 %all-to-all-start.1 = ((s32[32,1,2]{2,1,0:T(1,128)}), s32[32,1,2]{2,1,0:T(1,128)S(1)}, u32[]{:S(2)}, u32[]{:S(2)}) async-start(s32[32,1,2]{2,1,0:T(1,128)} %broadcast_in_dim.50), calls=%async_computation.1 | async-start | bytes 32768 | tf_op jit(solution)/shard_map/all_to_all | solution.py:15
  43.8 54.1 %all-to-all-start = ((bf16[32,256,128]{1,2,0:T(8,128)(2,1)}), bf16[32,256,128]{1,2,0:T(8,128)(2,1)S(1)}, u32[]{:S(2)}, u32[]{:S(2)}) async-start(bf16[32,256,128]{1,2,0:T(8,128)(2,1)} %broadcast_in_dim.45), calls=%async_computation | async-start | bytes 4194304 | tf_op jit(solution)/shard_map/all_to_all | solution.py:15
Sparse Core Ops, SparseCore 0:
  10.5 132.7 all-gather.2
  145.1 88.3 all-gather.4
where the time goes:
time: 262 us
  waiting for transfers between devices  184 us (70%)
  matrix products  29.2 us (11%)
  starting transfers between devices  20 us (8%)
  between operations  14.2 us (5%)
  local copies, waits for them, and re-layouts  12.7 us (5%)
    all_gather x1, waiting for transfers between devices, per_device(): entire_weight = lax.all_gather(up_weight, 'pop', axis=0, tiled=True)  84.6 us
    all_to_all x3, waiting for transfers between devices, sent_to_all(): return lax.all_to_all(copies, axis, split_axis=0, concat_axis=0, tiled=True)  52.3 us
    all_gather x1, waiting for transfers between devices, per_device(): piece = lax.all_gather(tokens, 'fsdp', axis=1, tiled=True)  45.3 us
    all_to_all x3, starting transfers between devices, sent_to_all(): return lax.all_to_all(copies, axis, split_axis=0, concat_axis=0, tiled=True)  19.9 us
    dot_general x1, matrix products, per_device(): jnp.dot(piece, entire_weight, preferred_element_type=jnp.float32)  17 us
    dot_general x1, matrix products, per_device(): low_sum = jnp.dot(piece, own_a.T, preferred_element_type=jnp.float32)  5.63 us
    gather x1, local copies, waits for them, and re-layouts, per_device(): picked_b = jnp.take(b_bank, flat_index, axis=0)  5.58 us
  transfers between devices with their start and end apart: 5, of which 5 were waited for; matrix products, arithmetic and copies ran while one was open for 9% of the time, Pallas kernels for 0%

commit v1 on v0

--- a/solution.py
+++ b/solution.py
@@ -56,7 +56,9 @@
     column_factor = jnp.repeat(noise_scale / math.sqrt(D * RANK) * own_signs, RANK)
     member_of_column = jnp.arange(own_width) // RANK
     row_count = tokens.shape[0]
-    entire_weight = lax.all_gather(up_weight, "pop", axis=0, tiled=True)
+    entire_weight = jnp.concatenate(
+        lax.all_to_all(jnp.stack([up_weight] * lax.axis_size("pop")), "pop", 0, 0), axis=0
+    )
     piece = lax.all_gather(tokens, "fsdp", axis=1, tiled=True)
     dense_sum = jnp.dot(piece, entire_weight, preferred_element_type=jnp.float32)
     low_sum = jnp.dot(piece, own_a.T, preferred_element_type=jnp.float32)

time: 262 us -> 460 us (1.76); the launches traced: 262 us -> 452 us
  waiting for transfers between devices: 184 us -> 314 us
  blocking collectives: 0 us -> 52.4 us
  local copies, waits for them, and re-layouts: 12.7 us -> 18.3 us
    all_to_all x0 -> x1, waiting for transfers between devices: none -> 139 us  [per_device(): lax.all_to_all(jnp.stack([up_weight] * lax.axis_size('pop')), 'pop', 0, 0)]
    all_gather x1, waiting for transfers between devices: 45.3 us -> 160 us  [per_device(): piece = lax.all_gather(tokens, 'fsdp', axis=1, tiled=True)]
    all_gather x1 -> x0, waiting for transfers between devices: 84.6 us -> none  [per_device(): entire_weight = lax.all_gather(up_weight, 'pop', axis=0, tiled=True)]
    all_to_all x0 -> x1, blocking collectives: none -> 52.4 us  [sent_to_all(): return lax.all_to_all(copies, axis, split_axis=0, concat_axis=0, tiled=True)]
    all_to_all x3 -> x2, waiting for transfers between devices: 52.3 us -> 13.5 us  [sent_to_all(): return lax.all_to_all(copies, axis, split_axis=0, concat_axis=0, tiled=True)]
    all_to_all x0 -> x1, starting transfers between devices: none -> 7.05 us  [per_device(): lax.all_to_all(jnp.stack([up_weight] * lax.axis_size('pop')), 'pop', 0, 0)]
    another operation x0 -> x1, local copies, waits for them, and re-layouts: none -> 6.84 us  [per_device(): jnp.stack([up_weight] * lax.axis_size('pop'))]
    all_to_all x3 -> x2, starting transfers between devices: 19.9 us -> 15.4 us  [sent_to_all(): return lax.all_to_all(copies, axis, split_axis=0, concat_axis=0, tiled=True)]
  transfers between devices with their start and end apart: 5 -> 4, of which waited for: 5 -> 4; matrix products, arithmetic and copies ran while one was open for 9% -> 4% of each run, Pallas kernels for 0% -> 0%
where the time goes in v1:
time: 460 us; the launch traced here: 452 us
  waiting for transfers between devices  314 us (68%)
  blocking collectives  52.4 us (11%)
  matrix products  28.7 us (6%)
  starting transfers between devices  22.7 us (5%)
  local copies, waits for them, and re-layouts  18.3 us (4%)
  between operations  14.2 us (3%)
    all_gather x1, waiting for transfers between devices, per_device(): piece = lax.all_gather(tokens, 'fsdp', axis=1, tiled=True)  160 us
    all_to_all x1, waiting for transfers between devices, per_device(): lax.all_to_all(jnp.stack([up_weight] * lax.axis_size('pop')), 'pop', 0, 0)  139 us
    all_to_all x1, blocking collectives, sent_to_all(): return lax.all_to_all(copies, axis, split_axis=0, concat_axis=0, tiled=True)  52.4 us
    dot_general x1, matrix products, per_device(): jnp.dot(piece, entire_weight, preferred_element_type=jnp.float32)  16.7 us
    all_to_all x2, starting transfers between devices, sent_to_all(): return lax.all_to_all(copies, axis, split_axis=0, concat_axis=0, tiled=True)  15.4 us
    all_to_all x2, waiting for transfers between devices, sent_to_all(): return lax.all_to_all(copies, axis, split_axis=0, concat_axis=0, tiled=True)  13.5 us
  transfers between devices with their start and end apart: 4, of which 4 were waited for; matrix products, arithmetic and copies ran while one was open for 4% of the time, Pallas kernels for 0%

profile of v1, /device:TPU:1, one launch (start us, length us, event | category | flops | bytes accessed | tf_op | source)
XLA Modules:
  0.0 452.4 jit_solution(1466194191540169315)
XLA Ops:
  7.2 0.0 copy-start
  7.2 0.0 copy-start.1
  7.2 1.3 broadcast_in_dim.51
  8.5 11.1 %all-to-all-start.3 = ((s32[32,1,2]{2,1,0:T(1,128)}), s32[32,1,2]{2,1,0:T(1,128)S(1)}, u32[]{:S(2)}, u32[]{:S(2)}) async-start(s32[32,1,2]{2,1,0:T(1,128)} %broadcast_in_dim.51), calls=%async_computation.3 | async-start | bytes 32768 | tf_op jit(solution)/shard_map/all_to_all | solution.py:15
  19.7 0.8 copy.15
  20.4 0.1 reshape.100
  20.5 0.1 reshape.99
  20.7 0.0 copy-done
  20.7 0.9 gather_fusion
  21.6 5.9 %all-to-all-done.3 = s32[32,1,2]{2,1,0:T(1,128)S(1)} async-done(((s32[32,1,2]{2,1,0:T(1,128)}), s32[32,1,2]{2,1,0:T(1,128)S(1)}, u32[]{:S(2)}, u32[]{:S(2)}) %all-to-all-start.3) | async-done | bytes 288 | tf_op jit(solution)/shard_map/all_to_all | solution.py:15
  27.4 1.3 broadcast_in_dim.50
  28.7 4.3 all-to-all-start.2
  33.0 0.1 broadcast_select_fusion.1
  33.1 0.1 copy.17
  33.2 7.6 %all-to-all-done.2 = s32[32,1,2]{2,1,0:T(1,128)S(1)} async-done(((s32[32,1,2]{2,1,0:T(1,128)}), s32[32,1,2]{2,1,0:T(1,128)S(1)}, u32[]{:S(2)}, u32[]{:S(2)}) %all-to-all-start.2) | async-done | bytes 288 | tf_op jit(solution)/shard_map/all_to_all | solution.py:15
  40.9 0.2 broadcast_in_dim.45
  41.1 52.4 %all_to_all.22 = bf16[32,256,128]{1,2,0:T(8,128)(2,1)S(1)} all-to-all(bf16[32,256,128]{1,2,0:T(8,128)(2,1)S(1)} %broadcast_in_dim.45), channel_id=1, replica_groups=mesh['pop'=32,'fsdp'=8] {'pop'}, dimensions={0} | all-to-all | bytes 4194304 | tf_op jit(solution)/shard_map/all_to_all | solution.py:15
  93.5 0.0 copy-done.1
  93.5 6.8 %stack.2 = bf16[32,128,1792]{2,1,0:T(8,128)(2,1)} broadcast(bf16[128,1792]{1,0:T(8,128)(2,1)S(1)} %copy-done.1), dimensions={1,2} | broadcast | bytes 15138816 | tf_op jit(solution)/shard_map/stack | solution.py:60
  100.4 0.0 copy-start.2
  100.4 7.1 %all-to-all-start = ((bf16[32,128,1792]{2,1,0:T(8,128)(2,1)}), bf16[32,128,1792]{2,1,0:T(8,128)(2,1)}, u32[]{:S(2)}, u32[]{:S(2)}) async-start(bf16[32,128,1792]{2,1,0:T(8,128)(2,1)} %stack.2), calls=%async_computation | async-start | bytes 29360128 | tf_op jit(solution)/shard_map/all_to_all | solution.py:60
  107.4 0.2 all-gather.2.cloned.1.call-start
  107.6 0.5 all-gather.2.cloned.1.call-update
  108.2 0.0 copy-done.2
  108.2 0.1 broadcast_in_dim.46
  108.3 0.1 mul.47
  108.3 5.6 %gather_fusion.1 = bf16[256,1792]{1,0:T(8,128)(2,1)} fusion(bf16[1024,1792]{1,0:T(8,128)(2,1)} %param.10, s32[1024]{0:T(1024)S(1)} %pad_clamp_fusion), kind=kCustom, calls=%fused_computation.1 | custom fusion | bytes 1836032 | tf_op jit(solution)/shard_map/jit(_take)/gather | solution.py:46
  113.9 1.3 broadcast_select_fusion
  115.3 0.1 convert_reduce_fusion.1
  115.3 0.1 convert_element_type.28
  115.4 0.5 broadcast.140
  116.0 0.7 reduce.7
  116.7 0.1 lt.62
  116.8 0.2 convert_reduce_fusion
  117.0 0.1 broadcast_in_dim.52
  117.0 0.1 mul.54
  117.1 1.9 fusion
  119.0 160.4 %all-gather.2.cloned.1.call-done = bf16[896,4096]{1,0:T(8,128)(2,1)} async-done(((bf16[896,512]{1,0:T(8,128)(2,1)}), bf16[896,4096]{1,0:T(8,128)(2,1)}) %all-gather.2.cloned.1.call-update) | async-done | bytes 7340048 | tf_op jit(solution)/shard_map/all_gather | solution.py:62
  279.4 5.6 %fusion.4 = f32[896,8]{0,1:T(8,128)S(1)} fusion(bf16[896,4096]{1,0:T(8,128)(2,1)} %all-gather.2.cloned.1.call-done, bf16[256,4096]{0,1:T(8,128)(2,1)S(1)} %bitcast.14, s32[]{:T(128)S(6)} %select_n.57, f32[8]{0:T(128)S(1)} %mul.47, s32[896]{0:T(1024)S(1)} %add_select_fusion, s32[8]{0:T(128)S(1)} %and_select_fusion), kind=kOutput, calls=%fused_computation.8 | convolution fusion | flops 58741760 | bytes 8422404 | tf_op jit(solution)/shard_map/dot_general | solution.py:64
  285.0 139.4 %all-to-all-done = bf16[32,128,1792]{2,1,0:T(8,128)(2,1)} async-done(((bf16[32,128,1792]{2,1,0:T(8,128)(2,1)}), bf16[32,128,1792]{2,1,0:T(8,128)(2,1)}, u32[]{:S(2)}, u32[]{:S(2)}) %all-to-all-start) | async-done | bytes 14680096 | tf_op jit(solution)/shard_map/all_to_all | solution.py:60
  424.4 16.7 %fusion.15 = f32[896,1792]{1,0:T(8,128)S(1)} fusion(bf16[896,4096]{1,0:T(8,128)(2,1)} %all-gather.2.cloned.1.call-done, bf16[4096,1792]{1,0:T(8,128)(2,1)} %bitcast), kind=kOutput, calls=%fused_computation.38 | convolution fusion | flops 13153337344 | bytes 28442624 | tf_op jit(solution)/shard_map/dot_general | solution.py:63
  441.1 4.4 add_convert_fusion
  (7 shorter events, 0.0 us)
Async XLA Ops:
  7.2 13.5 %copy-start = (bf16[1024,128]{1,0:T(8,128)(2,1)S(1)}, bf16[1024,128]{1,0:T(8,128)(2,1)}, u32[]{:S(2)}) copy-start(bf16[1024,128]{1,0:T(8,128)(2,1)} %param.9) | copy-start | bytes 786436
  7.2 86.3 %copy-start.1 = (bf16[128,1792]{1,0:T(8,128)(2,1)S(1)}, bf16[128,1792]{1,0:T(8,128)(2,1)}, u32[]{:S(2)}) copy-start(bf16[128,1792]{1,0:T(8,128)(2,1)} %param.8) | copy-start | bytes 1376260
  8.5 18.9 %all-to-all-start.3 = ((s32[32,1,2]{2,1,0:T(1,128)}), s32[32,1,2]{2,1,0:T(1,128)S(1)}, u32[]{:S(2)}, u32[]{:S(2)}) async-start(s32[32,1,2]{2,1,0:T(1,128)} %broadcast_in_dim.51), calls=%async_computation.3 | async-start | bytes 32768 | tf_op jit(solution)/shard_map/all_to_all | solution.py:15
  28.7 12.1 %all-to-all-start.2 = ((s32[32,1,2]{2,1,0:T(1,128)}), s32[32,1,2]{2,1,0:T(1,128)S(1)}, u32[]{:S(2)}, u32[]{:S(2)}) async-start(s32[32,1,2]{2,1,0:T(1,128)} %broadcast_in_dim.50), calls=%async_computation.2 | async-start | bytes 32768 | tf_op jit(solution)/shard_map/all_to_all | solution.py:15
  100.4 7.8 %copy-start.2 = (s32[2]{0:T(128)S(1)}, s32[2]{0:T(128)}, u32[]{:S(2)}) copy-start(s32[2]{0:T(128)} %param.12) | copy-start | bytes 28
  100.4 324.0 %all-to-all-start = ((bf16[32,128,1792]{2,1,0:T(8,128)(2,1)}), bf16[32,128,1792]{2,1,0:T(8,128)(2,1)}, u32[]{:S(2)}, u32[]{:S(2)}) async-start(bf16[32,128,1792]{2,1,0:T(8,128)(2,1)} %stack.2), calls=%async_computation | async-start | bytes 29360128 | tf_op jit(solution)/shard_map/all_to_all | solution.py:60
  107.4 172.0 %all-gather.2.cloned.1.call-start = ((), (), s32[]{:S(2)}) async-start(), calls=%async_computation.4 | async-start | bytes 8257536 | tf_op jit(solution)/shard_map/all_gather | solution.py:62
Sparse Core Ops, SparseCore 0:
  110.7 168.6 all-gather.1
